TPU v7x, 256 devices: a whole 4x4x8 slice. The times are simulated.
256 devices in a mesh: row: 16 (over z, x_hi), col: 16 (over x_lo, y, core).
Axes of the slice: x: 4 (x_hi: 2, x_lo: 2; x = x_hi * 2 + x_lo), y: 4, z: 8, core: 2. Of those that a mesh axis runs over, the one named last changes fastest.
Arguments:
- records: float32 [65536, 128], P(('row', 'col')), may hold values from -6 to 6
- move_face: int32 [65536], P(('row', 'col')), may hold values from 0 to 4, as said below
- move_slot: int32 [65536], P(('row', 'col')), may hold values from 0 to 255
- pattern_s: int32 [1024, 20], P(('row', 'col')), may hold values from 0 to 1, as said below
- pattern_x: int32 [1024, 20], P(('row', 'col')), may hold values from 0 to 1, as said below
- start_inverse: float32 [65536, 1280], P(('row', 'col')), may hold values from -0.04 to 1.25
Outputs:
- migrated: float32 [65536, 128], P(('row', 'col'))
- inverse: float32 [65536, 1280], P(('row', 'col'))
Inputs may be any that keep to these rules, and one draw needn't show every extreme that they name: `move_face`: on every device, among its 256 slots each of the faces 1, 2, 3, 4 is named at least once. `pattern_s`: symmetric as a relation between blocks; every block is coupled to itself. `pattern_x`: symmetric as a relation between blocks; ones wherever pattern_s has one.
All inputs are finite; a program needn't handle non-finite values.
Results may differ from a plain program's by a relative error of at most 0.0001.
Values sent between devices are 32-bit elements; how exact they have to be, the bound alone decides.
A program may use at most 64 MiB of HBM per device.

v0:
```python
import math

import jax
import jax.numpy as jnp
from jax import lax
from jax.experimental import pallas as pl
from jax.experimental.pallas import tpu as pltpu
from jax.sharding import PartitionSpec as P

BLK = 64
COUPLE_BASE = 0.2
F32 = jnp.float32
BF16 = jnp.bfloat16
MESH = pl.DeviceIdType.MESH

N = 256
FEAT = 128
CH = 4
CROWS = N // CH
WEST, EAST, NEAR, FAR = 0, 1, 2, 3
X0, P1, X1, P2 = 0, 1, 2, 3
RCH = 2
RROWS = N // RCH


def dot(a, b):
    return jnp.dot(a, b, preferred_element_type=F32)


def dot_nt(a, b):
    return lax.dot_general(a, b, (((1,), (1,)), ((), ())), preferred_element_type=F32)


def halves(x):
    high = x.astype(BF16)
    return high, (x - high.astype(F32)).astype(BF16)


def put_left(ref, x):
    high, low = halves(x)
    ref[:, 0:N] = high
    ref[:, N : 2 * N] = high
    ref[:, 2 * N : 3 * N] = low


def put_right(ref, x):
    high, low = halves(x)
    ref[0:N, :] = high
    ref[N : 2 * N, :] = low
    ref[2 * N : 3 * N, :] = high


def put_both(left, right, x):
    high, low = halves(x)
    left[:, 0:N] = high
    left[:, N : 2 * N] = high
    left[:, 2 * N : 3 * N] = low
    right[0:N, :] = high
    right[N : 2 * N, :] = low
    right[2 * N : 3 * N, :] = high


def make_kernel(n_row, n_col, coupling):
    def kernel(
        rec_hbm, face_ref, slot_ref, ps_ref, px_ref, x0_hbm,
        mig_out, inv_out,
        recs, pats, migs, opp, diag, own, xab, xba, outs,
        hot, split, mig_l, mig_r, rpat, sel, mask,
        eaa, eab, eba, ebb,
        xaa_l, x1aa_l, xab_l, xba_l, xbb_l,
        xaa_r, xab_r, xba_r, xbb_r, paa_r, pab_r, pba_r, pbb_r,
        loc, rec_s, rec_r, pat_s, pat_r, mig_s, mig_rs, opp_s, opp_r, dia_s, dia_r, out_s,
    ):
        r = lax.axis_index("row")
        c = lax.axis_index("col")
        odd = r % 2
        s = 1 - 2 * odd
        west = (r, (c + n_col - 1) % n_col)
        east = (r, (c + 1) % n_col)
        near = ((r + s + n_row) % n_row, c)
        far = ((r - s + n_row) % n_row, c)
        ahead = ((r + 2 * s + n_row) % n_row, c)
        behind = ((r - 2 * s + n_row) % n_row, c)
        group = (3, 4, 2 - odd, 1 + odd)
        direct = ((west, EAST), (east, WEST), (near, NEAR))

        def cols(q):
            return pl.ds(pl.multiple_of(q * N, N), N)

        local = []

        def fetch(src, dst):
            copy = pltpu.make_async_copy(src, dst, loc.at[len(local)])
            copy.start()
            local.append(copy)

        fetch(rec_hbm, recs.at[4])
        fetch(x0_hbm.at[:, 0:N], own.at[X0])
        for slot in range(4):
            fetch(x0_hbm.at[:, cols(group[slot])], xab.at[slot])

        pats[4] = jnp.zeros((8, 128), F32)
        pats[4, 0:4, 0:20] = jnp.where(ps_ref[...] > 0, 1.0, 0.0).astype(F32)
        pats[4, 4:8, 0:20] = jnp.where(px_ref[...] > 0, 1.0, 0.0).astype(F32)

        barrier = pltpu.get_barrier_semaphore()
        for other in (west, east, near, far, ahead, behind):
            pl.semaphore_signal(barrier, inc=1, device_id=other, device_id_type=MESH)
        pl.semaphore_wait(barrier, 6)

        sends = []

        def send(src, dst, ssem, rsem, device):
            copy = pltpu.make_async_remote_copy(
                src_ref=src, dst_ref=dst, send_sem=ssem, recv_sem=rsem, device_id=device, device_id_type=MESH
            )
            copy.start()
            sends.append(copy)

        def arrive(dst, ssem, rsem):
            pltpu.make_async_remote_copy(
                src_ref=dst, dst_ref=dst, send_sem=ssem, recv_sem=rsem, device_id=near, device_id_type=MESH
            ).wait_recv()

        def rrows(j):
            return pl.ds(j * RROWS, RROWS)

        def crows(j):
            return pl.ds(j * CROWS, CROWS)

        for j in range(RCH):
            for way in (2, 0, 1):
                device, theirs = direct[way]
                send(rec_hbm.at[rrows(j)], recs.at[theirs, rrows(j)], rec_s.at[way, j], rec_r.at[theirs, j], device)
        for way in (2, 0, 1):
            device, theirs = direct[way]
            send(pats.at[4], pats.at[theirs], pat_s.at[way], pat_r.at[theirs], device)
        for slot, (device, theirs) in ((FAR, (far, FAR)), (NEAR, (near, NEAR)), (WEST, direct[0]), (EAST, direct[1])):
            send(x0_hbm.at[:, cols(group[slot])], opp.at[theirs], opp_s.at[slot], opp_r.at[theirs], device)

        place = face_ref[...] * N + slot_ref[...]
        place = jnp.transpose(jnp.broadcast_to(place.astype(F32), (N, N)))
        lane = lax.broadcasted_iota(jnp.int32, (N, N), 1).astype(F32)
        for slot in range(5):
            q = 0 if slot == 4 else group[slot]
            first = (q * N * jnp.ones((1, 1), jnp.int32)).astype(F32)
            hot[:, slot * N : (slot + 1) * N] = jnp.where(place == lane + first, 1.0, 0.0).astype(BF16)

        row8 = lax.broadcasted_iota(jnp.int32, (N, 8), 0) // BLK
        col8 = lax.broadcasted_iota(jnp.int32, (N, 8), 1)
        spread_s = jnp.where(col8 == row8, 1.0, 0.0).astype(BF16)
        spread_x = jnp.where(col8 == row8 + 4, 1.0, 0.0).astype(BF16)
        row128 = lax.broadcasted_iota(jnp.int32, (N, 128), 0) // BLK
        col128 = lax.broadcasted_iota(jnp.int32, (N, 128), 1)
        for slot in range(5):
            q = 0 if slot == 4 else group[slot]
            sel[slot] = jnp.where(col128 == row128 + q * 4, 1.0, 0.0).astype(BF16)
        mine = pats[4].astype(BF16)
        rpat[0] = dot(spread_s, mine).astype(BF16)
        rpat[1] = dot(spread_x, mine).astype(BF16)

        for copy in local:
            copy.wait()

        def mask_slot(slot, carry):
            mask[slot] = dot_nt(rpat[1], sel[slot])
            mask[slot + 5] = dot_nt(sel[slot], rpat[1])
            block = xab[slot] * mask[slot]
            xab[slot] = block
            put_both(xab_l.at[slot], xab_r.at[slot], block)
            return carry

        mask[4] = dot_nt(rpat[1], sel[4])
        block = own[X0] * mask[4]
        own[X0] = block
        put_both(xaa_l, xaa_r, block)

        def three(slot):
            x = recs[slot]
            high = x.astype(BF16)
            rest = x - high.astype(F32)
            mid = rest.astype(BF16)
            low = (rest - mid.astype(F32)).astype(BF16)
            rows = pl.ds(pl.multiple_of(slot * N, N), N)
            split[rows, 0:FEAT] = high
            split[rows, FEAT : 2 * FEAT] = mid
            split[rows, 2 * FEAT : 3 * FEAT] = low

        three(4)
        lax.fori_loop(0, 4, mask_slot, 0)

        for j in range(RCH):
            arrive(recs.at[NEAR, rrows(j)], rec_s.at[3, j], rec_r.at[NEAR, j])
            send(recs.at[NEAR, rrows(j)], recs.at[FAR, rrows(j)], rec_s.at[3, j], rec_r.at[FAR, j], ahead)
        arrive(pats.at[NEAR], pat_s.at[3], pat_r.at[NEAR])
        send(pats.at[NEAR], pats.at[FAR], pat_s.at[3], pat_r.at[FAR], ahead)
        three(NEAR)
        for slot in (WEST, EAST, FAR):
            for j in range(RCH):
                arrive(recs.at[slot, rrows(j)], rec_s.at[3, j], rec_r.at[slot, j])
            three(slot)

        parts = dot(hot[...], split[...])
        migrated = (parts[:, 0:FEAT] + parts[:, FEAT : 2 * FEAT]) + parts[:, 2 * FEAT : 3 * FEAT]
        migs[4] = migrated
        for j in range(RCH):
            for way in (2, 0, 1):
                device, theirs = direct[way]
                send(migs.at[4, rrows(j)], migs.at[theirs, rrows(j)], mig_s.at[way, j], mig_rs.at[theirs, j], device)
        mig_copy = pltpu.make_async_copy(migs.at[4], mig_out, out_s.at[5])
        mig_copy.start()

        def put_mig(slot):
            high, low = halves(migs[slot])
            mig_l[slot, :, 0:FEAT] = high
            mig_l[slot, :, FEAT : 2 * FEAT] = high
            mig_l[slot, :, 2 * FEAT : 3 * FEAT] = low
            mig_r[slot, :, 0:FEAT] = high
            mig_r[slot, :, FEAT : 2 * FEAT] = low
            mig_r[slot, :, 2 * FEAT : 3 * FEAT] = high

        put_mig(4)
        put_left(eaa, dot_nt(mig_l[4], mig_r[4]) * coupling * dot_nt(rpat[0], sel[4]))

        for j in range(RCH):
            arrive(migs.at[NEAR, rrows(j)], mig_s.at[3, j], mig_rs.at[NEAR, j])
            send(migs.at[NEAR, rrows(j)], migs.at[FAR, rrows(j)], mig_s.at[3, j], mig_rs.at[FAR, j], ahead)

        def spread(kind):
            for j in range(CH):
                for way in (2, 0, 1):
                    device, theirs = direct[way]
                    send(
                        own.at[kind, crows(j)], diag.at[kind, theirs, crows(j)],
                        dia_s.at[kind, way, j], dia_r.at[kind, theirs, j], device,
                    )

        def take(kind, slot):
            def one(j, carry):
                rows = pl.ds(pl.multiple_of(j * CROWS, CROWS), CROWS)
                arrive(diag.at[kind, slot, rows], dia_s.at[kind, 3, j], dia_r.at[kind, slot, j])
                return carry

            lax.fori_loop(0, CH, one, 0)

        def forward(kind):
            for j in range(CH):
                arrive(diag.at[kind, NEAR, crows(j)], dia_s.at[kind, 3, j], dia_r.at[kind, NEAR, j])
                send(
                    diag.at[kind, NEAR, crows(j)], diag.at[kind, FAR, crows(j)],
                    dia_s.at[kind, 3, j], dia_r.at[kind, FAR, j], ahead,
                )

        spread(X0)

        def couple(slot):
            put_mig(slot)
            put_left(eab.at[slot], dot_nt(mig_l[4], mig_r[slot]) * coupling * dot_nt(rpat[0], sel[slot]))
            put_left(eba.at[slot], dot_nt(mig_l[slot], mig_r[4]) * coupling * dot_nt(sel[slot], rpat[0]))
            theirs = dot_nt(dot(spread_s, pats[slot].astype(BF16)).astype(BF16), sel[4])
            put_left(ebb.at[slot], dot_nt(mig_l[slot], mig_r[slot]) * coupling * theirs)

        def arrive_mig(slot):
            arrive(pats.at[slot], pat_s.at[3], pat_r.at[slot])
            for j in range(RCH):
                arrive(migs.at[slot, rrows(j)], mig_s.at[3, j], mig_rs.at[slot, j])

        def take_opp(slot):
            arrive(opp.at[slot], opp_s.at[slot], opp_r.at[slot])
            block = opp[slot] * mask[slot + 5]
            xba[slot] = block
            put_both(xba_l.at[slot], xba_r.at[slot], block)

        def couple_side(slot, carry):
            arrive_mig(slot)
            couple(slot)
            take_opp(slot)
            own[P1] += dot(eab[slot], xba_r[slot])
            return carry

        own[P1] = own[X0] + dot(eaa[...], xaa_r[...])
        lax.fori_loop(0, 2, couple_side, 0)
        couple(NEAR)
        take_opp(NEAR)
        own[P1] += dot(eab[NEAR], xba_r[NEAR])
        arrive_mig(FAR)
        couple(FAR)
        take_opp(FAR)
        block = (own[P1] + dot(eab[FAR], xba_r[FAR])) * mask[4]
        own[P1] = block
        spread(P1)
        put_right(paa_r, block)

        def back_product(slot):
            block = xba[slot] + dot(ebb[slot], xba_r[slot]) + dot(eba[slot], xaa_r[...])
            put_right(pba_r.at[slot], block * mask[slot + 5])

        def first_diag(slot, carry):
            back_product(slot)
            own[X1] -= dot(xab_l[slot], pba_r[slot])
            return carry

        own[X1] = 2.0 * own[X0] - dot(xaa_l[...], paa_r[...])
        lax.fori_loop(0, 4, first_diag, 0)
        block = own[X1] * mask[4]
        own[X1] = block
        spread(X1)
        put_both(x1aa_l, xaa_r, block)

        forward(X0)
        own[P2] = block + dot(eaa[...], xaa_r[...])

        def take_x0(slot):
            put_both(xbb_l.at[slot], xbb_r.at[slot], diag[X0, slot])

        def next_back(slot):
            take_x0(slot)
            block = 2.0 * xba[slot] - dot(xbb_l[slot], pba_r[slot]) - dot(xba_l[slot], paa_r[...])
            block = block * mask[slot + 5]
            xba[slot] = block
            put_right(xba_r.at[slot], block)
            own[P2] += dot(eab[slot], xba_r[slot])

        def next_side(slot, carry):
            take(X0, slot)
            next_back(slot)
            return carry

        lax.fori_loop(0, 2, next_side, 0)
        next_back(NEAR)
        take(X0, FAR)
        next_back(FAR)
        block = own[P2] * mask[4]
        own[P2] = block
        spread(P2)
        put_right(paa_r, block)

        outs[4] = 2.0 * own[X1] - dot(x1aa_l[...], paa_r[...])

        def ahead_product(slot, carry):
            block = xab[slot] + dot(eaa[...], xab_r[slot]) + dot(eab[slot], xbb_r[slot])
            put_right(pab_r.at[slot], block * mask[slot])
            xab[slot] = 2.0 * xab[slot] - dot(xaa_l[...], pab_r[slot])
            back_product(slot)
            return carry

        lax.fori_loop(0, 4, ahead_product, 0)

        def first_ahead(slot):
            put_right(pbb_r.at[slot], diag[P1, slot])
            block = (xab[slot] - dot(xab_l[slot], pbb_r[slot])) * mask[slot]
            xab[slot] = block
            put_both(xab_l.at[slot], xab_r.at[slot], block)
            outs[4] -= dot(xab_l[slot], pba_r[slot])

        def first_side(slot, carry):
            take(P1, slot)
            first_ahead(slot)
            return carry

        forward(P1)
        lax.fori_loop(0, 2, first_side, 0)
        first_ahead(NEAR)
        take(P1, FAR)
        first_ahead(FAR)
        outs[4] = outs[4] * mask[4]
        out_copies = [pltpu.make_async_copy(outs.at[4], inv_out.at[:, 0:N], out_s.at[4])]
        out_copies[0].start()

        def second_product(slot):
            put_right(xbb_r.at[slot], diag[X1, slot])
            block = xab[slot] + dot(eaa[...], xab_r[slot]) + dot(eab[slot], xbb_r[slot])
            put_right(pab_r.at[slot], block * mask[slot])
            xab[slot] = 2.0 * xab[slot] - dot(x1aa_l[...], pab_r[slot])

        def second_side(slot, carry):
            take(X1, slot)
            second_product(slot)
            return carry

        forward(X1)
        lax.fori_loop(0, 2, second_side, 0)
        second_product(NEAR)
        take(X1, FAR)
        second_product(FAR)

        def finish(slot):
            put_right(pbb_r.at[slot], diag[P2, slot])
            outs[slot] = (xab[slot] - dot(xab_l[slot], pbb_r[slot])) * mask[slot]
            copy = pltpu.make_async_copy(outs.at[slot], inv_out.at[:, cols(group[slot])], out_s.at[slot])
            copy.start()
            out_copies.append(copy)

        forward(P2)
        take(P2, WEST)
        finish(WEST)
        take(P2, EAST)
        finish(EAST)
        finish(NEAR)
        take(P2, FAR)
        finish(FAR)

        for copy in sends:
            copy.wait_send()
        mig_copy.wait()
        for copy in out_copies:
            copy.wait()

    return kernel


def solution(mesh):
    n_row, n_col = mesh.shape["row"], mesh.shape["col"]
    coupling = COUPLE_BASE / math.sqrt(5 * FEAT * N)
    vmem = pl.BlockSpec(memory_space=pltpu.VMEM)
    hbm = pl.BlockSpec(memory_space=pl.ANY)
    dma = pltpu.SemaphoreType.DMA

    def f32(*shape):
        return pltpu.VMEM(shape, F32)

    def bf16(*shape):
        return pltpu.VMEM(shape, BF16)

    left = bf16(N, 3 * N)
    left4 = bf16(4, N, 3 * N)
    right = bf16(3 * N, N)
    right4 = bf16(4, 3 * N, N)

    def body(records, move_face, move_slot, pattern_s, pattern_x, start_inverse):
        return pl.pallas_call(
            make_kernel(n_row, n_col, coupling),
            out_shape=(
                jax.ShapeDtypeStruct((N, FEAT), F32),
                jax.ShapeDtypeStruct((N, 5 * N), F32),
            ),
            in_specs=[hbm, vmem, vmem, vmem, vmem, hbm],
            out_specs=(hbm, hbm),
            scratch_shapes=[
                f32(5, N, FEAT), f32(5, 8, 128), f32(5, N, FEAT), f32(4, N, N), f32(4, 4, N, N), f32(4, N, N),
                f32(4, N, N), f32(4, N, N), f32(5, N, N),
                bf16(N, 5 * N), bf16(5 * N, 3 * FEAT), bf16(5, N, 3 * FEAT), bf16(5, N, 3 * FEAT),
                bf16(2, N, 128), bf16(5, N, 128), f32(9, N, N),
                left, left4, left4, left4,
                left, left, left4, left4, left4,
                right, right4, right4, right4, right, right4, right4, right4,
                dma((6,)), dma((4, RCH)), dma((4, RCH)), dma((4,)), dma((4,)), dma((4, RCH)), dma((4, RCH)),
                dma((4,)), dma((4,)), dma((4, 4, CH)), dma((4, 4, CH)), dma((6,)),
            ],
            compiler_params=pltpu.CompilerParams(
                collective_id=0, has_side_effects=True, vmem_limit_bytes=56 << 20
            ),
            cost_estimate=pl.CostEstimate(flops=8 * 10**9, bytes_accessed=3 * 2**20, transcendentals=0),
            name="hotelling",
        )(
            records,
            move_face.reshape(1, N),
            move_slot.reshape(1, N),
            pattern_s,
            pattern_x,
            start_inverse,
        )

    split = P(("row", "col"))
    wide = P(("row", "col"), None)
    return jax.shard_map(
        body,
        mesh=mesh,
        in_specs=(wide, split, split, wide, wide, wide),
        out_specs=(wide, wide),
        check_vma=False,
    )
```

profile of v0, /device:TPU:2, one launch (start us, length us, event | category | flops | bytes accessed | tf_op | source)
XLA Modules:
  0.0 84.7 jit_solution(4381436200065743610)
XLA Ops:
  0.6 80.1 %hotelling.1 = (f32[256,128]{1,0:T(8,128)}, f32[256,1280]{1,0:T(8,128)}) custom-call(f32[256,128]{1,0:T(8,128)} %rec_hbm.1, s32[1,256]{1,0:T(1,128)} %bitcast.2, s32[1,256]{1,0:T(1,128)} %bitcast.3, s32[4,20]{1,0:T(4,128)} %ps_ref.1, s32[4,20]{1,0:T(4,128)} %px_ref.1, f32[256,1280]{1,0:T(8,128)} %x0_hbm.1), custom_call_target="tpu_custom_call" | custom-call | flops 8000000000 | bytes 3145728 | tf_op jit(solution)/shard_map/hotelling/pallas_call | solution.py:431
  80.7 1.6 %copy.10 = f32[256,128]{1,0:T(8,128)} copy(f32[256,128]{1,0:T(8,128)} %get-tuple-element.4) | data formatting | bytes 262144
  82.3 2.5 %copy.11 = f32[256,1280]{1,0:T(8,128)} copy(f32[256,1280]{1,0:T(8,128)} %get-tuple-element.5) | data formatting | bytes 2621440
where the time goes:
time: 86 us; the launch traced here: 84.7 us
  Pallas kernels  80.1 us (93%)
  local copies, waits for them, and re-layouts  4.02 us (5%)
    pallas_call x1, Pallas kernels, body(): pl.pallas_call(make_kernel(n_row, n_col, coupling), out_shape=(jax.ShapeD...  80.1 us
    unnamed x2, local copies, waits for them, and re-layouts  4.02 us

commit v1 on v0

--- a/solution.py
+++ b/solution.py
@@ -21,6 +21,8 @@
 X0, P1, X1, P2 = 0, 1, 2, 3
 RCH = 2
 RROWS = N // RCH
+DETOUR = {X0: (0, 1), P1: (0, 1), X1: (0, 1), P2: ()}
+RELAY = 4
 
 
 def dot(a, b):
@@ -83,6 +85,17 @@
         behind = ((r - 2 * s + n_row) % n_row, c)
         group = (3, 4, 2 - odd, 1 + odd)
         direct = ((west, EAST), (east, WEST), (near, NEAR))
+        at_first, at_last = c % 8 == 0, c % 8 == 7
+        is_relay = (c % 8 == 2) | (c % 8 == 5)
+        back2, on2 = (r, (c + n_col - 2) % n_col), (r, (c + 2) % n_col)
+        back3, on3 = (r, (c + n_col - 3) % n_col), (r, (c + 3) % n_col)
+        detour = (
+            ((r, jnp.where(at_first, on2[1], west[1])), jnp.where(at_first, RELAY, EAST)),
+            ((r, jnp.where(at_last, back2[1], east[1])), jnp.where(at_last, RELAY, WEST)),
+        )
+        forth = c % 2 == 1
+        goal = (r, jnp.where(forth, on3[1], back3[1]))
+        goal_slot = jnp.where(forth, WEST, EAST)
 
         def cols(q):
             return pl.ds(pl.multiple_of(q * N, N), N)
@@ -104,29 +117,44 @@
         pats[4, 4:8, 0:20] = jnp.where(px_ref[...] > 0, 1.0, 0.0).astype(F32)
 
         barrier = pltpu.get_barrier_semaphore()
-        for other in (west, east, near, far, ahead, behind):
+        for other in (west, east, near, far, ahead, behind, back2, on2, back3, on3):
             pl.semaphore_signal(barrier, inc=1, device_id=other, device_id_type=MESH)
-        pl.semaphore_wait(barrier, 6)
-
-        sends = []
+        pl.semaphore_wait(barrier, 10)
 
         def send(src, dst, ssem, rsem, device):
             copy = pltpu.make_async_remote_copy(
                 src_ref=src, dst_ref=dst, send_sem=ssem, recv_sem=rsem, device_id=device, device_id_type=MESH
             )
             copy.start()
-            sends.append(copy)
 
         def arrive(dst, ssem, rsem):
             pltpu.make_async_remote_copy(
                 src_ref=dst, dst_ref=dst, send_sem=ssem, recv_sem=rsem, device_id=near, device_id_type=MESH
             ).wait_recv()
 
+        def sent(src, ssem):
+            pltpu.make_async_remote_copy(
+                src_ref=src, dst_ref=src, send_sem=ssem, recv_sem=loc.at[0], device_id=near, device_id_type=MESH
+            ).wait_send()
+
         def rrows(j):
             return pl.ds(j * RROWS, RROWS)
 
         def crows(j):
-            return pl.ds(j * CROWS, CROWS)
+            return pl.ds(pl.multiple_of(j * CROWS, CROWS), CROWS)
+
+        relayed = []
+
+        def relay(src, dst, ssem, here, there):
+            copy = pltpu.make_async_remote_copy(
+                src_ref=src, dst_ref=dst, send_sem=ssem, recv_sem=there, device_id=goal, device_id_type=MESH
+            )
+            relayed.append(copy)
+
+            @pl.when(is_relay)
+            def _():
+                arrive(src, ssem, here)
+                copy.start()
 
         for j in range(RCH):
             for way in (2, 0, 1):
@@ -135,7 +163,7 @@
         for way in (2, 0, 1):
             device, theirs = direct[way]
             send(pats.at[4], pats.at[theirs], pat_s.at[way], pat_r.at[theirs], device)
-        for slot, (device, theirs) in ((FAR, (far, FAR)), (NEAR, (near, NEAR)), (WEST, direct[0]), (EAST, direct[1])):
+        for slot, (device, theirs) in ((FAR, (far, FAR)), (NEAR, (near, NEAR)), (WEST, detour[0]), (EAST, detour[1])):
             send(x0_hbm.at[:, cols(group[slot])], opp.at[theirs], opp_s.at[slot], opp_r.at[theirs], device)
 
         place = face_ref[...] * N + slot_ref[...]
@@ -219,6 +247,8 @@
             mig_r[slot, :, FEAT : 2 * FEAT] = low
             mig_r[slot, :, 2 * FEAT : 3 * FEAT] = high
 
+        relay(opp.at[RELAY], opp.at[goal_slot], opp_s.at[RELAY], opp_r.at[RELAY], opp_r.at[goal_slot])
+
         put_mig(4)
         put_left(eaa, dot_nt(mig_l[4], mig_r[4]) * coupling * dot_nt(rpat[0], sel[4]))
 
@@ -229,7 +259,7 @@
         def spread(kind):
             for j in range(CH):
                 for way in (2, 0, 1):
-                    device, theirs = direct[way]
+                    device, theirs = detour[way] if way < 2 and j in DETOUR[kind] else direct[way]
                     send(
                         own.at[kind, crows(j)], diag.at[kind, theirs, crows(j)],
                         dia_s.at[kind, way, j], dia_r.at[kind, theirs, j], device,
@@ -243,19 +273,27 @@
 
             lax.fori_loop(0, CH, one, 0)
 
-        def forward(kind):
-            for j in range(CH):
-                arrive(diag.at[kind, NEAR, crows(j)], dia_s.at[kind, 3, j], dia_r.at[kind, NEAR, j])
-                send(
-                    diag.at[kind, NEAR, crows(j)], diag.at[kind, FAR, crows(j)],
-                    dia_s.at[kind, 3, j], dia_r.at[kind, FAR, j], ahead,
+        def relay_diag(kind):
+            for j in DETOUR[kind]:
+                relay(
+                    diag.at[kind, RELAY, crows(j)], diag.at[kind, goal_slot, crows(j)],
+                    dia_s.at[kind, RELAY, j], dia_r.at[kind, RELAY, j], dia_r.at[kind, goal_slot, j],
                 )
+
+        def forward(kind, j):
+            arrive(diag.at[kind, NEAR, crows(j)], dia_s.at[kind, 3, j], dia_r.at[kind, NEAR, j])
+            send(
+                diag.at[kind, NEAR, crows(j)], diag.at[kind, FAR, crows(j)],
+                dia_s.at[kind, 3, j], dia_r.at[kind, FAR, j], ahead,
+            )
 
         spread(X0)
 
         def couple(slot):
             put_mig(slot)
             put_left(eab.at[slot], dot_nt(mig_l[4], mig_r[slot]) * coupling * dot_nt(rpat[0], sel[slot]))
+
+        def couple_back(slot):
             put_left(eba.at[slot], dot_nt(mig_l[slot], mig_r[4]) * coupling * dot_nt(sel[slot], rpat[0]))
             theirs = dot_nt(dot(spread_s, pats[slot].astype(BF16)).astype(BF16), sel[4])
             put_left(ebb.at[slot], dot_nt(mig_l[slot], mig_r[slot]) * coupling * theirs)
@@ -296,8 +334,10 @@
             put_right(pba_r.at[slot], block * mask[slot + 5])
 
         def first_diag(slot, carry):
+            couple_back(slot)
             back_product(slot)
             own[X1] -= dot(xab_l[slot], pba_r[slot])
+            forward(X0, slot)
             return carry
 
         own[X1] = 2.0 * own[X0] - dot(xaa_l[...], paa_r[...])
@@ -307,7 +347,7 @@
         spread(X1)
         put_both(x1aa_l, xaa_r, block)
 
-        forward(X0)
+        relay_diag(X0)
         own[P2] = block + dot(eaa[...], xaa_r[...])
 
         def take_x0(slot):
@@ -327,7 +367,9 @@
             return carry
 
         lax.fori_loop(0, 2, next_side, 0)
+        forward(P1, 0)
         next_back(NEAR)
+        forward(P1, 1)
         take(X0, FAR)
         next_back(FAR)
         block = own[P2] * mask[4]
@@ -335,6 +377,9 @@
         spread(P2)
         put_right(paa_r, block)
 
+        forward(P1, 2)
+        forward(P1, 3)
+        relay_diag(P1)
         outs[4] = 2.0 * own[X1] - dot(x1aa_l[...], paa_r[...])
 
         def ahead_product(slot, carry):
@@ -342,9 +387,11 @@
             put_right(pab_r.at[slot], block * mask[slot])
             xab[slot] = 2.0 * xab[slot] - dot(xaa_l[...], pab_r[slot])
             back_product(slot)
+            forward(X1, slot)
             return carry
 
         lax.fori_loop(0, 4, ahead_product, 0)
+        relay_diag(X1)
 
         def first_ahead(slot):
             put_right(pbb_r.at[slot], diag[P1, slot])
@@ -358,7 +405,6 @@
             first_ahead(slot)
             return carry
 
-        forward(P1)
         lax.fori_loop(0, 2, first_side, 0)
         first_ahead(NEAR)
         take(P1, FAR)
@@ -378,11 +424,14 @@
             second_product(slot)
             return carry
 
-        forward(X1)
         lax.fori_loop(0, 2, second_side, 0)
+        forward(P2, 0)
         second_product(NEAR)
+        forward(P2, 1)
         take(X1, FAR)
+        forward(P2, 2)
         second_product(FAR)
+        forward(P2, 3)
 
         def finish(slot):
             put_right(pbb_r.at[slot], diag[P2, slot])
@@ -391,7 +440,6 @@
             copy.start()
             out_copies.append(copy)
 
-        forward(P2)
         take(P2, WEST)
         finish(WEST)
         take(P2, EAST)
@@ -400,13 +448,37 @@
         take(P2, FAR)
         finish(FAR)
 
-        for copy in sends:
-            copy.wait_send()
+        def sent_way(way, carry):
+            sent(pats.at[4], pat_s.at[way])
+            sent(opp.at[way], opp_s.at[way])
+            for j in range(RCH):
+                sent(recs.at[4, rrows(j)], rec_s.at[way, j])
+                sent(migs.at[4, rrows(j)], mig_s.at[way, j])
+
+            def sent_kind(kind, carry):
+                for j in range(CH):
+                    sent(own.at[kind, crows(j)], dia_s.at[kind, way, j])
+                return carry
+
+            return lax.fori_loop(0, 4, sent_kind, carry)
+
+        lax.fori_loop(0, 4, sent_way, 0)
+
+        @pl.when(is_relay)
+        def _():
+            for copy in relayed:
+                copy.wait_send()
+
         mig_copy.wait()
         for copy in out_copies:
             copy.wait()
 
     return kernel
+
+
+def hand_over(mig_in, inv_in, mig_out, inv_out):
+    mig_out[...] = mig_in[...]
+    inv_out[...] = inv_in[...]
 
 
 def solution(mesh):
@@ -428,16 +500,14 @@
     right4 = bf16(4, 3 * N, N)
 
     def body(records, move_face, move_slot, pattern_s, pattern_x, start_inverse):
-        return pl.pallas_call(
+        shapes = (jax.ShapeDtypeStruct((N, FEAT), F32), jax.ShapeDtypeStruct((N, 5 * N), F32))
+        results = pl.pallas_call(
             make_kernel(n_row, n_col, coupling),
-            out_shape=(
-                jax.ShapeDtypeStruct((N, FEAT), F32),
-                jax.ShapeDtypeStruct((N, 5 * N), F32),
-            ),
+            out_shape=shapes,
             in_specs=[hbm, vmem, vmem, vmem, vmem, hbm],
             out_specs=(hbm, hbm),
             scratch_shapes=[
-                f32(5, N, FEAT), f32(5, 8, 128), f32(5, N, FEAT), f32(4, N, N), f32(4, 4, N, N), f32(4, N, N),
+                f32(5, N, FEAT), f32(5, 8, 128), f32(5, N, FEAT), f32(5, N, N), f32(4, 5, N, N), f32(4, N, N),
                 f32(4, N, N), f32(4, N, N), f32(5, N, N),
                 bf16(N, 5 * N), bf16(5 * N, 3 * FEAT), bf16(5, N, 3 * FEAT), bf16(5, N, 3 * FEAT),
                 bf16(2, N, 128), bf16(5, N, 128), f32(9, N, N),
@@ -445,7 +515,7 @@
                 left, left, left4, left4, left4,
                 right, right4, right4, right4, right, right4, right4, right4,
                 dma((6,)), dma((4, RCH)), dma((4, RCH)), dma((4,)), dma((4,)), dma((4, RCH)), dma((4, RCH)),
-                dma((4,)), dma((4,)), dma((4, 4, CH)), dma((4, 4, CH)), dma((6,)),
+                dma((5,)), dma((5,)), dma((4, 5, CH)), dma((4, 5, CH)), dma((6,)),
             ],
             compiler_params=pltpu.CompilerParams(
                 collective_id=0, has_side_effects=True, vmem_limit_bytes=56 << 20
@@ -460,6 +530,13 @@
             pattern_x,
             start_inverse,
         )
+        return pl.pallas_call(
+            hand_over,
+            out_shape=shapes,
+            in_specs=[vmem, vmem],
+            out_specs=(vmem, vmem),
+            name="hand_over",
+        )(*results)
 
     split = P(("row", "col"))
     wide = P(("row", "col"), None)

time: 86 us -> 75.7 us (0.88)
  Pallas kernels: 80.1 us -> 74.2 us
  local copies, waits for them, and re-layouts: 4.02 us -> 0 us
    pallas_call x1 -> x2, Pallas kernels: 80.1 us -> 74.2 us  [the longest x1 71.7 us: body(): pl.pallas_call(make_kernel(n_row, n_col, coupling), out_shape=shapes, in_...]
    unnamed x2 -> x0, local copies, waits for them, and re-layouts: 4.02 us -> none
where the time goes in v1:
time: 75.7 us; the launch traced here: 74.8 us
  Pallas kernels  74.2 us (98%)
    pallas_call x1, Pallas kernels, body(): pl.pallas_call(make_kernel(n_row, n_col, coupling), out_shape=shapes, in_...  71.7 us
    pallas_call x1, Pallas kernels, body(): pl.pallas_call(hand_over, out_shape=shapes, in_specs=[vmem, vmem], out_sp...  2.55 us

profile of v1, /device:TPU:2, one launch (start us, length us, event | category | flops | bytes accessed | tf_op | source)
XLA Modules:
  0.0 74.8 jit_solution(6632084330528976775)
XLA Ops:
  0.6 71.7 %hotelling.1 = (f32[256,128]{1,0:T(8,128)}, f32[256,1280]{1,0:T(8,128)}) custom-call(f32[256,128]{1,0:T(8,128)} %rec_hbm.1, s32[1,256]{1,0:T(1,128)} %bitcast.2, s32[1,256]{1,0:T(1,128)} %bitcast.3, s32[4,20]{1,0:T(4,128)} %ps_ref.1, s32[4,20]{1,0:T(4,128)} %px_ref.1, f32[256,1280]{1,0:T(8,128)} %x0_hbm.1), custom_call_target="tpu_custom_call" | custom-call | flops 8000000000 | bytes 3145728 | tf_op jit(solution)/shard_map/hotelling/pallas_call | solution.py:504
  72.3 2.5 %hand_over.1 = (f32[256,128]{1,0:T(8,128)}, f32[256,1280]{1,0:T(8,128)}) custom-call(f32[256,128]{1,0:T(8,128)} %get-tuple-element.4.mig_in, f32[256,1280]{1,0:T(8,128)} %get-tuple-element.5.inv_in), custom_call_target="tpu_custom_call" | custom-call | tf_op jit(solution)/shard_map/hand_over/pallas_call | solution.py:533

commit v2 on v1

--- a/solution.py
+++ b/solution.py
@@ -21,7 +21,7 @@
 X0, P1, X1, P2 = 0, 1, 2, 3
 RCH = 2
 RROWS = N // RCH
-DETOUR = {X0: (0, 1), P1: (0, 1), X1: (0, 1), P2: ()}
+DETOUR = {X0: (0, 1), P1: (0, 1), X1: (0, 1), P2: (0, 1)}
 RELAY = 4
 
 
@@ -66,8 +66,8 @@
     def kernel(
         rec_hbm, face_ref, slot_ref, ps_ref, px_ref, x0_hbm,
         mig_out, inv_out,
-        recs, pats, migs, opp, diag, own, xab, xba, outs,
-        hot, split, mig_l, mig_r, rpat, sel, mask,
+        recs, pats, migs, opp, diag, own, xab, xba, pab, outs,
+        hot, split, mig_l, mig_r, rpat, sel, mask, link,
         eaa, eab, eba, ebb,
         xaa_l, x1aa_l, xab_l, xba_l, xbb_l,
         xaa_r, xab_r, xba_r, xbb_r, paa_r, pab_r, pba_r, pbb_r,
@@ -163,9 +163,6 @@
         for way in (2, 0, 1):
             device, theirs = direct[way]
             send(pats.at[4], pats.at[theirs], pat_s.at[way], pat_r.at[theirs], device)
-        for slot, (device, theirs) in ((FAR, (far, FAR)), (NEAR, (near, NEAR)), (WEST, detour[0]), (EAST, detour[1])):
-            send(x0_hbm.at[:, cols(group[slot])], opp.at[theirs], opp_s.at[slot], opp_r.at[theirs], device)
-
         place = face_ref[...] * N + slot_ref[...]
         place = jnp.transpose(jnp.broadcast_to(place.astype(F32), (N, N)))
         lane = lax.broadcasted_iota(jnp.int32, (N, N), 1).astype(F32)
@@ -187,18 +184,25 @@
         rpat[0] = dot(spread_s, mine).astype(BF16)
         rpat[1] = dot(spread_x, mine).astype(BF16)
 
+        for j in range(RCH):
+            sent(recs.at[4, rrows(j)], rec_s.at[2, j])
+        for slot, (device, theirs) in ((FAR, (far, FAR)), (NEAR, (near, NEAR)), (WEST, detour[0]), (EAST, detour[1])):
+            send(x0_hbm.at[:, cols(group[slot])], opp.at[theirs], opp_s.at[slot], opp_r.at[theirs], device)
+
+
         for copy in local:
             copy.wait()
 
-        def mask_slot(slot, carry):
+        for slot in range(5):
             mask[slot] = dot_nt(rpat[1], sel[slot])
+            link[slot] = dot_nt(rpat[0], sel[slot]) * coupling
+        for slot in range(4):
             mask[slot + 5] = dot_nt(sel[slot], rpat[1])
+            link[slot + 5] = dot_nt(sel[slot], rpat[0]) * coupling
+        for slot in range(4):
             block = xab[slot] * mask[slot]
             xab[slot] = block
             put_both(xab_l.at[slot], xab_r.at[slot], block)
-            return carry
-
-        mask[4] = dot_nt(rpat[1], sel[4])
         block = own[X0] * mask[4]
         own[X0] = block
         put_both(xaa_l, xaa_r, block)
@@ -215,7 +219,6 @@
             split[rows, 2 * FEAT : 3 * FEAT] = low
 
         three(4)
-        lax.fori_loop(0, 4, mask_slot, 0)
 
         for j in range(RCH):
             arrive(recs.at[NEAR, rrows(j)], rec_s.at[3, j], rec_r.at[NEAR, j])
@@ -227,6 +230,38 @@
             for j in range(RCH):
                 arrive(recs.at[slot, rrows(j)], rec_s.at[3, j], rec_r.at[slot, j])
             three(slot)
+            arrive(pats.at[slot], pat_s.at[3], pat_r.at[slot])
+
+        def spread(kind):
+            for j in range(CH):
+                for way in (2, 0, 1):
+                    device, theirs = detour[way] if way < 2 and j in DETOUR[kind] else direct[way]
+                    send(
+                        own.at[kind, crows(j)], diag.at[kind, theirs, crows(j)],
+                        dia_s.at[kind, way, j], dia_r.at[kind, theirs, j], device,
+                    )
+
+        def relay_diag(kind):
+            for j in DETOUR[kind]:
+                relay(
+                    diag.at[kind, RELAY, crows(j)], diag.at[kind, goal_slot, crows(j)],
+                    dia_s.at[kind, RELAY, j], dia_r.at[kind, RELAY, j], dia_r.at[kind, goal_slot, j],
+                )
+
+        def take(kind, slot):
+            for j in range(CH):
+                arrive(diag.at[kind, slot, crows(j)], dia_s.at[kind, 3, j], dia_r.at[kind, slot, j])
+
+        def forward(kind, j):
+            arrive(diag.at[kind, NEAR, crows(j)], dia_s.at[kind, 3, j], dia_r.at[kind, NEAR, j])
+            send(
+                diag.at[kind, NEAR, crows(j)], diag.at[kind, FAR, crows(j)],
+                dia_s.at[kind, 3, j], dia_r.at[kind, FAR, j], ahead,
+            )
+
+        def forward_all(kind):
+            for j in range(CH):
+                forward(kind, j)
 
         parts = dot(hot[...], split[...])
         migrated = (parts[:, 0:FEAT] + parts[:, FEAT : 2 * FEAT]) + parts[:, 2 * FEAT : 3 * FEAT]
@@ -249,220 +284,182 @@
 
         relay(opp.at[RELAY], opp.at[goal_slot], opp_s.at[RELAY], opp_r.at[RELAY], opp_r.at[goal_slot])
 
+        for slot in range(4):
+            link[slot + 9] = dot_nt(dot(spread_s, pats[slot].astype(BF16)).astype(BF16), sel[4]) * coupling
         put_mig(4)
-        put_left(eaa, dot_nt(mig_l[4], mig_r[4]) * coupling * dot_nt(rpat[0], sel[4]))
+        put_left(eaa, dot_nt(mig_l[4], mig_r[4]) * link[4])
+        own[P1] = own[X0] + dot(eaa[...], xaa_r[...])
+        for slot in range(4):
+            pab[slot] = xab[slot] + dot(eaa[...], xab_r[slot])
 
         for j in range(RCH):
             arrive(migs.at[NEAR, rrows(j)], mig_s.at[3, j], mig_rs.at[NEAR, j])
             send(migs.at[NEAR, rrows(j)], migs.at[FAR, rrows(j)], mig_s.at[3, j], mig_rs.at[FAR, j], ahead)
-
-        def spread(kind):
-            for j in range(CH):
-                for way in (2, 0, 1):
-                    device, theirs = detour[way] if way < 2 and j in DETOUR[kind] else direct[way]
-                    send(
-                        own.at[kind, crows(j)], diag.at[kind, theirs, crows(j)],
-                        dia_s.at[kind, way, j], dia_r.at[kind, theirs, j], device,
-                    )
-
-        def take(kind, slot):
-            def one(j, carry):
-                rows = pl.ds(pl.multiple_of(j * CROWS, CROWS), CROWS)
-                arrive(diag.at[kind, slot, rows], dia_s.at[kind, 3, j], dia_r.at[kind, slot, j])
-                return carry
-
-            lax.fori_loop(0, CH, one, 0)
-
-        def relay_diag(kind):
-            for j in DETOUR[kind]:
-                relay(
-                    diag.at[kind, RELAY, crows(j)], diag.at[kind, goal_slot, crows(j)],
-                    dia_s.at[kind, RELAY, j], dia_r.at[kind, RELAY, j], dia_r.at[kind, goal_slot, j],
-                )
-
-        def forward(kind, j):
-            arrive(diag.at[kind, NEAR, crows(j)], dia_s.at[kind, 3, j], dia_r.at[kind, NEAR, j])
-            send(
-                diag.at[kind, NEAR, crows(j)], diag.at[kind, FAR, crows(j)],
-                dia_s.at[kind, 3, j], dia_r.at[kind, FAR, j], ahead,
-            )
-
         spread(X0)
 
-        def couple(slot):
-            put_mig(slot)
-            put_left(eab.at[slot], dot_nt(mig_l[4], mig_r[slot]) * coupling * dot_nt(rpat[0], sel[slot]))
-
-        def couple_back(slot):
-            put_left(eba.at[slot], dot_nt(mig_l[slot], mig_r[4]) * coupling * dot_nt(sel[slot], rpat[0]))
-            theirs = dot_nt(dot(spread_s, pats[slot].astype(BF16)).astype(BF16), sel[4])
-            put_left(ebb.at[slot], dot_nt(mig_l[slot], mig_r[slot]) * coupling * theirs)
+        def couple(*slots):
+            for slot in slots:
+                put_mig(slot)
+            for slot in slots:
+                put_left(eab.at[slot], dot_nt(mig_l[4], mig_r[slot]) * link[slot])
+
+        def couple_back(*slots):
+            for slot in slots:
+                put_left(eba.at[slot], dot_nt(mig_l[slot], mig_r[4]) * link[slot + 5])
+                put_left(ebb.at[slot], dot_nt(mig_l[slot], mig_r[slot]) * link[slot + 9])
 
         def arrive_mig(slot):
-            arrive(pats.at[slot], pat_s.at[3], pat_r.at[slot])
             for j in range(RCH):
                 arrive(migs.at[slot, rrows(j)], mig_s.at[3, j], mig_rs.at[slot, j])
 
-        def take_opp(slot):
-            arrive(opp.at[slot], opp_s.at[slot], opp_r.at[slot])
-            block = opp[slot] * mask[slot + 5]
-            xba[slot] = block
-            put_both(xba_l.at[slot], xba_r.at[slot], block)
-
-        def couple_side(slot, carry):
-            arrive_mig(slot)
-            couple(slot)
-            take_opp(slot)
-            own[P1] += dot(eab[slot], xba_r[slot])
-            return carry
-
-        own[P1] = own[X0] + dot(eaa[...], xaa_r[...])
-        lax.fori_loop(0, 2, couple_side, 0)
-        couple(NEAR)
-        take_opp(NEAR)
-        own[P1] += dot(eab[NEAR], xba_r[NEAR])
+        def take_opp(*slots):
+            for slot in slots:
+                arrive(opp.at[slot], opp_s.at[slot], opp_r.at[slot])
+            for slot in slots:
+                block = opp[slot] * mask[slot + 5]
+                xba[slot] = block
+                put_both(xba_l.at[slot], xba_r.at[slot], block)
+
+        def back_product(*slots):
+            for slot in slots:
+                block = xba[slot] + dot(ebb[slot], xba_r[slot]) + dot(eba[slot], xaa_r[...])
+                put_right(pba_r.at[slot], block * mask[slot + 5])
+
+        arrive_mig(WEST)
+        arrive_mig(EAST)
+        couple(WEST, EAST, NEAR)
+        take_opp(WEST, EAST, NEAR, FAR)
+        own[P1] = own[P1] + dot(eab[WEST], xba_r[WEST]) + dot(eab[EAST], xba_r[EAST]) + dot(eab[NEAR], xba_r[NEAR])
+        couple_back(WEST, EAST)
+        back_product(WEST, EAST)
+        own[X1] = 2.0 * own[X0] - dot(xab_l[WEST], pba_r[WEST]) - dot(xab_l[EAST], pba_r[EAST])
+
+        relay_diag(X0)
         arrive_mig(FAR)
         couple(FAR)
-        take_opp(FAR)
         block = (own[P1] + dot(eab[FAR], xba_r[FAR])) * mask[4]
         own[P1] = block
         spread(P1)
         put_right(paa_r, block)
-
-        def back_product(slot):
-            block = xba[slot] + dot(ebb[slot], xba_r[slot]) + dot(eba[slot], xaa_r[...])
-            put_right(pba_r.at[slot], block * mask[slot + 5])
-
-        def first_diag(slot, carry):
-            couple_back(slot)
-            back_product(slot)
-            own[X1] -= dot(xab_l[slot], pba_r[slot])
-            forward(X0, slot)
-            return carry
-
-        own[X1] = 2.0 * own[X0] - dot(xaa_l[...], paa_r[...])
-        lax.fori_loop(0, 4, first_diag, 0)
-        block = own[X1] * mask[4]
+        couple_back(NEAR, FAR)
+        back_product(NEAR, FAR)
+        block = own[X1] - dot(xab_l[NEAR], pba_r[NEAR]) - dot(xab_l[FAR], pba_r[FAR]) - dot(xaa_l[...], paa_r[...])
+        block = block * mask[4]
         own[X1] = block
         spread(X1)
         put_both(x1aa_l, xaa_r, block)
-
-        relay_diag(X0)
-        own[P2] = block + dot(eaa[...], xaa_r[...])
-
-        def take_x0(slot):
-            put_both(xbb_l.at[slot], xbb_r.at[slot], diag[X0, slot])
-
-        def next_back(slot):
-            take_x0(slot)
-            block = 2.0 * xba[slot] - dot(xbb_l[slot], pba_r[slot]) - dot(xba_l[slot], paa_r[...])
-            block = block * mask[slot + 5]
-            xba[slot] = block
-            put_right(xba_r.at[slot], block)
-            own[P2] += dot(eab[slot], xba_r[slot])
-
-        def next_side(slot, carry):
-            take(X0, slot)
-            next_back(slot)
-            return carry
-
-        lax.fori_loop(0, 2, next_side, 0)
-        forward(P1, 0)
-        next_back(NEAR)
-        forward(P1, 1)
+        forward_all(X0)
+
+        def next_back(*slots):
+            for slot in slots:
+                put_both(xbb_l.at[slot], xbb_r.at[slot], diag[X0, slot])
+            for slot in slots:
+                block = 2.0 * xba[slot] - dot(xbb_l[slot], pba_r[slot]) - dot(xba_l[slot], paa_r[...])
+                block = block * mask[slot + 5]
+                xba[slot] = block
+                put_right(xba_r.at[slot], block)
+
+        take(X0, WEST)
+        take(X0, EAST)
+        next_back(WEST, EAST, NEAR)
+        own[P2] = (
+            own[X1] + dot(eaa[...], xaa_r[...])
+            + dot(eab[WEST], xba_r[WEST]) + dot(eab[EAST], xba_r[EAST]) + dot(eab[NEAR], xba_r[NEAR])
+        )
         take(X0, FAR)
         next_back(FAR)
-        block = own[P2] * mask[4]
+        block = (own[P2] + dot(eab[FAR], xba_r[FAR])) * mask[4]
         own[P2] = block
         spread(P2)
         put_right(paa_r, block)
 
-        forward(P1, 2)
-        forward(P1, 3)
+        def ahead_product(*slots):
+            for slot in slots:
+                block = pab[slot] + dot(eab[slot], xbb_r[slot])
+                put_right(pab_r.at[slot], block * mask[slot])
+            for slot in slots:
+                xab[slot] = 2.0 * xab[slot] - dot(xaa_l[...], pab_r[slot])
+
         relay_diag(P1)
+        forward_all(P1)
+        ahead_product(WEST, EAST, NEAR, FAR)
+        back_product(WEST, EAST, NEAR, FAR)
         outs[4] = 2.0 * own[X1] - dot(x1aa_l[...], paa_r[...])
-
-        def ahead_product(slot, carry):
-            block = xab[slot] + dot(eaa[...], xab_r[slot]) + dot(eab[slot], xbb_r[slot])
-            put_right(pab_r.at[slot], block * mask[slot])
-            xab[slot] = 2.0 * xab[slot] - dot(xaa_l[...], pab_r[slot])
-            back_product(slot)
-            forward(X1, slot)
-            return carry
-
-        lax.fori_loop(0, 4, ahead_product, 0)
         relay_diag(X1)
-
-        def first_ahead(slot):
-            put_right(pbb_r.at[slot], diag[P1, slot])
-            block = (xab[slot] - dot(xab_l[slot], pbb_r[slot])) * mask[slot]
-            xab[slot] = block
-            put_both(xab_l.at[slot], xab_r.at[slot], block)
-            outs[4] -= dot(xab_l[slot], pba_r[slot])
-
-        def first_side(slot, carry):
-            take(P1, slot)
-            first_ahead(slot)
-            return carry
-
-        lax.fori_loop(0, 2, first_side, 0)
-        first_ahead(NEAR)
+        forward_all(X1)
+
+        def first_ahead(*slots):
+            for slot in slots:
+                put_right(pbb_r.at[slot], diag[P1, slot])
+            for slot in slots:
+                block = (xab[slot] - dot(xab_l[slot], pbb_r[slot])) * mask[slot]
+                xab[slot] = block
+                put_both(xab_l.at[slot], xab_r.at[slot], block)
+
+        take(P1, WEST)
+        take(P1, EAST)
+        first_ahead(WEST, EAST, NEAR)
         take(P1, FAR)
         first_ahead(FAR)
-        outs[4] = outs[4] * mask[4]
+        block = outs[4] - dot(xab_l[WEST], pba_r[WEST]) - dot(xab_l[EAST], pba_r[EAST])
+        outs[4] = (block - dot(xab_l[NEAR], pba_r[NEAR]) - dot(xab_l[FAR], pba_r[FAR])) * mask[4]
         out_copies = [pltpu.make_async_copy(outs.at[4], inv_out.at[:, 0:N], out_s.at[4])]
         out_copies[0].start()
 
-        def second_product(slot):
-            put_right(xbb_r.at[slot], diag[X1, slot])
-            block = xab[slot] + dot(eaa[...], xab_r[slot]) + dot(eab[slot], xbb_r[slot])
-            put_right(pab_r.at[slot], block * mask[slot])
-            xab[slot] = 2.0 * xab[slot] - dot(x1aa_l[...], pab_r[slot])
-
-        def second_side(slot, carry):
-            take(X1, slot)
-            second_product(slot)
-            return carry
-
-        lax.fori_loop(0, 2, second_side, 0)
-        forward(P2, 0)
-        second_product(NEAR)
-        forward(P2, 1)
+        def second_product(*slots):
+            for slot in slots:
+                put_right(xbb_r.at[slot], diag[X1, slot])
+            for slot in slots:
+                block = xab[slot] + dot(eaa[...], xab_r[slot]) + dot(eab[slot], xbb_r[slot])
+                put_right(pab_r.at[slot], block * mask[slot])
+            for slot in slots:
+                xab[slot] = 2.0 * xab[slot] - dot(x1aa_l[...], pab_r[slot])
+
+        take(X1, WEST)
+        take(X1, EAST)
+        second_product(WEST, EAST, NEAR)
+        relay_diag(P2)
+        forward_all(P2)
         take(X1, FAR)
-        forward(P2, 2)
         second_product(FAR)
-        forward(P2, 3)
-
-        def finish(slot):
-            put_right(pbb_r.at[slot], diag[P2, slot])
-            outs[slot] = (xab[slot] - dot(xab_l[slot], pbb_r[slot])) * mask[slot]
-            copy = pltpu.make_async_copy(outs.at[slot], inv_out.at[:, cols(group[slot])], out_s.at[slot])
-            copy.start()
-            out_copies.append(copy)
+
+        def finish(*slots):
+            for slot in slots:
+                put_right(pbb_r.at[slot], diag[P2, slot])
+            for slot in slots:
+                outs[slot] = (xab[slot] - dot(xab_l[slot], pbb_r[slot])) * mask[slot]
+            for slot in slots:
+                copy = pltpu.make_async_copy(outs.at[slot], inv_out.at[:, cols(group[slot])], out_s.at[slot])
+                copy.start()
+                out_copies.append(copy)
 
         take(P2, WEST)
-        finish(WEST)
         take(P2, EAST)
-        finish(EAST)
-        finish(NEAR)
+        finish(WEST, EAST, NEAR)
         take(P2, FAR)
         finish(FAR)
+
+        def sent_diag(way):
+            def sent_kind(kind, carry):
+                for j in range(CH):
+                    sent(own.at[kind, crows(j)], dia_s.at[kind, way, j])
+                return carry
+
+            lax.fori_loop(0, 4, sent_kind, 0)
 
         def sent_way(way, carry):
             sent(pats.at[4], pat_s.at[way])
             sent(opp.at[way], opp_s.at[way])
             for j in range(RCH):
+                sent(migs.at[4, rrows(j)], mig_s.at[way, j])
+            return carry
+
+        lax.fori_loop(0, 4, sent_way, 0)
+        for way in (0, 1, 3):
+            for j in range(RCH):
                 sent(recs.at[4, rrows(j)], rec_s.at[way, j])
-                sent(migs.at[4, rrows(j)], mig_s.at[way, j])
-
-            def sent_kind(kind, carry):
-                for j in range(CH):
-                    sent(own.at[kind, crows(j)], dia_s.at[kind, way, j])
-                return carry
-
-            return lax.fori_loop(0, 4, sent_kind, carry)
-
-        lax.fori_loop(0, 4, sent_way, 0)
+        for way in range(4):
+            sent_diag(way)
 
         @pl.when(is_relay)
         def _():
@@ -508,9 +505,9 @@
             out_specs=(hbm, hbm),
             scratch_shapes=[
                 f32(5, N, FEAT), f32(5, 8, 128), f32(5, N, FEAT), f32(5, N, N), f32(4, 5, N, N), f32(4, N, N),
-                f32(4, N, N), f32(4, N, N), f32(5, N, N),
+                f32(4, N, N), f32(4, N, N), f32(4, N, N), f32(5, N, N),
                 bf16(N, 5 * N), bf16(5 * N, 3 * FEAT), bf16(5, N, 3 * FEAT), bf16(5, N, 3 * FEAT),
-                bf16(2, N, 128), bf16(5, N, 128), f32(9, N, N),
+                bf16(2, N, 128), bf16(5, N, 128), f32(9, N, N), f32(13, N, N),
                 left, left4, left4, left4,
                 left, left, left4, left4, left4,
                 right, right4, right4, right4, right, right4, right4, right4,

time: 75.7 us -> 73.7 us (0.974)
  Pallas kernels: 74.2 us -> 72.8 us
    pallas_call x1, Pallas kernels: 71.7 us -> 70.3 us  [body(): pl.pallas_call(make_kernel(n_row, n_col, coupling), out_shape=shapes, in_...]
where the time goes in v2:
time: 73.7 us; the launch traced here: 73.5 us
  Pallas kernels  72.8 us (99%)
    pallas_call x1, Pallas kernels, body(): pl.pallas_call(make_kernel(n_row, n_col, coupling), out_shape=shapes, in_...  70.3 us
    pallas_call x1, Pallas kernels, body(): pl.pallas_call(hand_over, out_shape=shapes, in_specs=[vmem, vmem], out_sp...  2.55 us

profile of v2, /device:TPU:2, one launch (start us, length us, event | category | flops | bytes accessed | tf_op | source)
XLA Modules:
  0.0 73.5 jit_solution(9483656065842812510)
XLA Ops:
  0.6 70.3 %hotelling.1 = (f32[256,128]{1,0:T(8,128)}, f32[256,1280]{1,0:T(8,128)}) custom-call(f32[256,128]{1,0:T(8,128)} %rec_hbm.1, s32[1,256]{1,0:T(1,128)} %bitcast.2, s32[1,256]{1,0:T(1,128)} %bitcast.3, s32[4,20]{1,0:T(4,128)} %ps_ref.1, s32[4,20]{1,0:T(4,128)} %px_ref.1, f32[256,1280]{1,0:T(8,128)} %x0_hbm.1), custom_call_target="tpu_custom_call" | custom-call | flops 8000000000 | bytes 3145728 | tf_op jit(solution)/shard_map/hotelling/pallas_call | solution.py:501
  70.9 2.5 %hand_over.1 = (f32[256,128]{1,0:T(8,128)}, f32[256,1280]{1,0:T(8,128)}) custom-call(f32[256,128]{1,0:T(8,128)} %get-tuple-element.4.mig_in, f32[256,1280]{1,0:T(8,128)} %get-tuple-element.5.inv_in), custom_call_target="tpu_custom_call" | custom-call | tf_op jit(solution)/shard_map/hand_over/pallas_call | solution.py:530

commit v3 on v2

--- a/solution.py
+++ b/solution.py
@@ -21,7 +21,7 @@
 X0, P1, X1, P2 = 0, 1, 2, 3
 RCH = 2
 RROWS = N // RCH
-DETOUR = {X0: (0, 1), P1: (0, 1), X1: (0, 1), P2: (0, 1)}
+DETOUR = {X0: (0, 1), P1: (0, 1), X1: (0, 1), P2: (0,)}
 RELAY = 4
 
 
@@ -163,6 +163,9 @@
         for way in (2, 0, 1):
             device, theirs = direct[way]
             send(pats.at[4], pats.at[theirs], pat_s.at[way], pat_r.at[theirs], device)
+        for slot, (device, theirs) in ((FAR, (far, FAR)), (NEAR, (near, NEAR)), (WEST, detour[0]), (EAST, detour[1])):
+            send(x0_hbm.at[:, cols(group[slot])], opp.at[theirs], opp_s.at[slot], opp_r.at[theirs], device)
+
         place = face_ref[...] * N + slot_ref[...]
         place = jnp.transpose(jnp.broadcast_to(place.astype(F32), (N, N)))
         lane = lax.broadcasted_iota(jnp.int32, (N, N), 1).astype(F32)
@@ -186,10 +189,6 @@
 
         for j in range(RCH):
             sent(recs.at[4, rrows(j)], rec_s.at[2, j])
-        for slot, (device, theirs) in ((FAR, (far, FAR)), (NEAR, (near, NEAR)), (WEST, detour[0]), (EAST, detour[1])):
-            send(x0_hbm.at[:, cols(group[slot])], opp.at[theirs], opp_s.at[slot], opp_r.at[theirs], device)
-
-
         for copy in local:
             copy.wait()
 
@@ -366,6 +365,7 @@
             own[X1] + dot(eaa[...], xaa_r[...])
             + dot(eab[WEST], xba_r[WEST]) + dot(eab[EAST], xba_r[EAST]) + dot(eab[NEAR], xba_r[NEAR])
         )
+        relay_diag(P1)
         take(X0, FAR)
         next_back(FAR)
         block = (own[P2] + dot(eab[FAR], xba_r[FAR])) * mask[4]
@@ -380,13 +380,12 @@
             for slot in slots:
                 xab[slot] = 2.0 * xab[slot] - dot(xaa_l[...], pab_r[slot])
 
-        relay_diag(P1)
         forward_all(P1)
         ahead_product(WEST, EAST, NEAR, FAR)
         back_product(WEST, EAST, NEAR, FAR)
         outs[4] = 2.0 * own[X1] - dot(x1aa_l[...], paa_r[...])
+        forward_all(X1)
         relay_diag(X1)
-        forward_all(X1)
 
         def first_ahead(*slots):
             for slot in slots:
@@ -418,8 +417,8 @@
         take(X1, WEST)
         take(X1, EAST)
         second_product(WEST, EAST, NEAR)
+        forward_all(P2)
         relay_diag(P2)
-        forward_all(P2)
         take(X1, FAR)
         second_product(FAR)
 

time: 73.7 us -> 72.9 us (0.989)
  no operation moved by 1% of the time
where the time goes in v3:
time: 72.9 us; the launch traced here: 72.8 us
  Pallas kernels  72.2 us (99%)
    pallas_call x1, Pallas kernels, body(): pl.pallas_call(make_kernel(n_row, n_col, coupling), out_shape=shapes, in_...  69.6 us
    pallas_call x1, Pallas kernels, body(): pl.pallas_call(hand_over, out_shape=shapes, in_specs=[vmem, vmem], out_sp...  2.55 us

profile of v3, /device:TPU:2, one launch (start us, length us, event | category | flops | bytes accessed | tf_op | source)
XLA Modules:
  0.0 72.8 jit_solution(8663605948237355118)
XLA Ops:
  0.6 69.6 %hotelling.1 = (f32[256,128]{1,0:T(8,128)}, f32[256,1280]{1,0:T(8,128)}) custom-call(f32[256,128]{1,0:T(8,128)} %rec_hbm.1, s32[1,256]{1,0:T(1,128)} %bitcast.2, s32[1,256]{1,0:T(1,128)} %bitcast.3, s32[4,20]{1,0:T(4,128)} %ps_ref.1, s32[4,20]{1,0:T(4,128)} %px_ref.1, f32[256,1280]{1,0:T(8,128)} %x0_hbm.1), custom_call_target="tpu_custom_call" | custom-call | flops 8000000000 | bytes 3145728 | tf_op jit(solution)/shard_map/hotelling/pallas_call | solution.py:500
  70.2 2.5 %hand_over.1 = (f32[256,128]{1,0:T(8,128)}, f32[256,1280]{1,0:T(8,128)}) custom-call(f32[256,128]{1,0:T(8,128)} %get-tuple-element.4.mig_in, f32[256,1280]{1,0:T(8,128)} %get-tuple-element.5.inv_in), custom_call_target="tpu_custom_call" | custom-call | tf_op jit(solution)/shard_map/hand_over/pallas_call | solution.py:529
